TPU v7x, 32 devices: a whole 2x2x4 slice. The times are simulated.
32 devices in a mesh: section: 4 (over y, core), expert: 8 (over z, x).
Axes of the slice: x: 2, y: 2, z: 4, core: 2. Of those that a mesh axis runs over, the one named last changes fastest.
Arguments:
- out_grad: bfloat16 [4, 1024, 7168], P('section', 'expert'), may hold values from -6 to 6
- router_weight: bfloat16 [4, 7168, 2], P('section'), may hold values from -0.25 to 0.25
- down_weight: bfloat16 [4, 2048, 7168], P('section', 'expert'), may hold values from -0.1875 to 0.1875
- hidden_saved: bfloat16 [4, 8, 8, 32, 256], P('section', 'expert'), may hold values from -1.5 to 1.5
- slot_token: int32 [4, 8, 2, 32], P('section', 'expert'), may hold values from 0 to 127, as said below
- slot_count: int32 [4, 8, 2], P('section', 'expert'), may hold values from 8 to 32, as said below
- slot_gate: float32 [4, 8, 2, 32], P('section', 'expert'), may hold values from 0.02 to 1
Outputs:
- down_grad: bfloat16 [4, 2048, 7168], P('section', 'expert')
- hidden_grad: bfloat16 [4, 8, 8, 32, 256], P('section', 'expert')
- passed_grad: bfloat16 [4, 1024, 7168], P('section', 'expert')
Inputs may be any that keep to these rules, and one draw needn't show every extreme that they name: `slot_token`: within each block the used slots name distinct tokens; entries at slots from the count onward are ignored. `slot_count`: in every section one expert has 32 used slots in the block of every source device.
All inputs are finite; a program needn't handle non-finite values.
Results may differ from a plain program's by a relative error of at most 0.015.
Values may be sent and summed in bfloat16 or wider, within the bound.
A program may use at most 128 MiB of HBM per device.

v0:
```python
import jax
import jax.numpy as jnp
from jax import lax
from jax.sharding import PartitionSpec as P


def passed_along(value, axis, steps):
    count = lax.axis_size(axis)
    initial, last = (max(0, -steps), min(count, count - steps))
    return lax.ppermute(value, axis, [(source, source + steps) for source in range(initial, last)])


def shards(out_grad, router_weight, down_weight, hidden_saved, slot_token, slot_count, slot_gate):
    high = lax.Precision.HIGHEST
    grad = out_grad[0]
    tokens = slot_token[0, 0]
    counts = slot_count[0, 0]
    gates = slot_gate[0, 0]
    experts, capacity = tokens.shape
    width = grad.shape[1]
    group = lax.axis_size("expert") // experts
    slots = lax.broadcasted_iota(jnp.int32, (experts, capacity), 1)
    live = slots < counts[:, None]
    gate_live = jnp.where(live, gates, jnp.float32(0.0))
    rows = jnp.where(live[..., None], grad[tokens], jnp.zeros((), grad.dtype))
    gate_sent = jnp.broadcast_to(gate_live[:, None], (experts, group, capacity)).reshape(
        experts * group, capacity
    )
    sent = jnp.broadcast_to(rows[:, None], (experts, group, capacity, width)).reshape(
        experts * group, capacity, width
    )
    got_rows, got_gate = (
        lax.all_to_all(sent, "expert", split_axis=0, concat_axis=0, tiled=True),
        lax.all_to_all(
            gate_sent.astype(jnp.bfloat16), "expert", split_axis=0, concat_axis=0, tiled=True
        ).astype(gate_sent.dtype),
    )
    w_block = down_weight[0]
    held = hidden_saved[0, 0]
    proj = jnp.einsum("scd,hd->sch", got_rows, w_block, preferred_element_type=jnp.float32)
    hidden_grad = (got_gate[..., None] * proj).astype(jnp.bfloat16)
    partial_value = jnp.sum(held.astype(jnp.float32) * proj, axis=-1)
    scaled = (got_gate[..., None] * got_rows.astype(jnp.float32)).astype(jnp.bfloat16)
    down_grad = jnp.einsum("sch,scd->hd", held, scaled, preferred_element_type=jnp.float32).astype(
        jnp.bfloat16
    )
    returned = lax.all_to_all(partial_value, "expert", split_axis=0, concat_axis=0, tiled=True)
    gate_grad = returned.reshape(experts, group, capacity).sum(axis=1)
    tok_count = grad.shape[0]
    positions = lax.broadcasted_iota(jnp.int32, (experts, capacity, tok_count), 2)
    match = jnp.where(
        (tokens[..., None] == positions) & live[..., None], jnp.float32(1.0), jnp.float32(0.0)
    )
    logit_grad = jnp.einsum("ec,ect->te", gate_grad, match, precision=high)
    input_grad = grad.astype(jnp.float32) + jnp.dot(
        logit_grad, router_weight[0].astype(jnp.float32).T, precision=high
    )
    passed = passed_along(input_grad.astype(jnp.bfloat16), "section", -1)
    return (down_grad[None], hidden_grad[None, None], passed[None])


def solution(mesh):
    return jax.shard_map(
        shards,
        mesh=mesh,
        in_specs=(
            P("section", "expert", None),
            P("section", None, None),
            P("section", "expert", None),
            P("section", "expert", None, None, None),
            P("section", "expert", None, None),
            P("section", "expert", None),
            P("section", "expert", None, None),
        ),
        out_specs=(
            P("section", "expert", None),
            P("section", "expert", None, None, None),
            P("section", "expert", None),
        ),
        check_vma=False,
    )
```

profile of v0, /device:TPU:1, one launch (start us, length us, event | category | flops | bytes accessed | tf_op | source)
XLA Modules:
  0.0 148.2 jit_solution(3844219321596100005)
XLA Ops:
  0.6 0.0 copy-start
  0.6 0.8 fusion.17
  1.4 0.6 copy.12
  2.0 6.4 %all-to-all-start = ((bf16[8,1,32]{2,1,0:T(2,128)(2,1)}), bf16[8,1,32]{2,1,0:T(2,128)(2,1)S(1)}, u32[]{:S(2)}, u32[]{:S(2)}) async-start(bf16[8,1,32]{2,1,0:T(2,128)(2,1)} %copy.12), calls=%async_computation | async-start | bytes 8192 | tf_op jit(solution)/shard_map/all_to_all | solution.py:34
  8.4 0.7 iota_compare_fusion.1
  9.1 0.7 compare_select_fusion
  9.8 0.1 reshape.117
  9.9 3.7 %gather_fusion = bf16[64,7168]{1,0:T(8,128)(2,1)S(1)} fusion(bf16[128,7168]{1,0:T(8,128)(2,1)} %bitcast.52, s32[1024]{0:T(1024)S(1)} %pad_clamp_fusion), kind=kCustom, calls=%fused_computation | custom fusion | bytes 1835264 | tf_op jit(solution)/shard_map/gather | solution.py:25
  13.6 0.1 broadcast_select_fusion
  13.7 0.0 all-to-all-done
  13.7 2.3 %broadcast_in_dim.54 = bf16[2,4,32,7168]{3,2,1,0:T(8,128)(2,1)} broadcast(bf16[2,32,7168]{2,1,0:T(8,128)(2,1)S(1)} %broadcast_select_fusion), dimensions={0,2,3} | broadcast | bytes 4587520 | tf_op jit(solution)/shard_map/broadcast_in_dim | solution.py:29
  16.0 0.0 copy-start.3
  16.0 5.6 %all-to-all-start.1 = ((bf16[8,32,7168]{2,1,0:T(8,128)(2,1)}), bf16[8,32,7168]{2,1,0:T(8,128)(2,1)}, u32[]{:S(2)}, u32[]{:S(2)}) async-start(bf16[8,32,7168]{2,1,0:T(8,128)(2,1)} %bitcast.53), calls=%async_computation.1 | async-start | bytes 7340032 | tf_op jit(solution)/shard_map/all_to_all | solution.py:33
  21.5 80.6 %all-to-all-done.1 = bf16[8,32,7168]{2,1,0:T(8,128)(2,1)} async-done(((bf16[8,32,7168]{2,1,0:T(8,128)(2,1)}), bf16[8,32,7168]{2,1,0:T(8,128)(2,1)}, u32[]{:S(2)}, u32[]{:S(2)}) %all-to-all-start.1) | async-done | bytes 3670048 | tf_op jit(solution)/shard_map/all_to_all | solution.py:33
  102.2 0.0 copy-done.3
  102.2 0.0 copy-start.2
  102.2 0.0 copy-start.1
  102.2 5.1 %multiply_reduce_fusion = (f32[8,32]{1,0:T(8,128)S(1)}, bf16[1,1,8,32,256]{4,3,2,1,0:T(8,128)(2,1)}) fusion(bf16[1,1,8,32,256]{4,3,2,1,0:T(8,128)(2,1)S(1)} %copy-done.3, f32[8,32]{1,0:T(8,128)S(1)} %bitcast.58, bf16[8,32,7168]{2,1,0:T(8,128)(2,1)} %all-to-all-done.1, bf16[1,256,7168]{2,1,0:T(8,128)(2,1)} %param.9), kind=kOutput, calls=%fused_computation.11 | convolution fusion | flops 939851520 | bytes 7604224 | tf_op jit(solution)/shard_map/scd,hd->sch/dot_general | solution.py:40
  107.2 10.3 %all_to_all.20 = f32[8,1,32]{2,1,0:T(1,128)S(1)} all-to-all(f32[8,1,32]{2,1,0:T(1,128)S(1)} %bitcast.60), channel_id=1, replica_groups=mesh['section'=4,'expert'=8] {'expert'}, dimensions={0} | all-to-all | bytes 2048 | tf_op jit(solution)/shard_map/all_to_all | solution.py:47
  117.6 0.0 copy-done.2
  117.6 0.2 fusion.8
  117.8 0.0 copy-done
  117.9 0.0 copy-done.1
  117.9 3.0 %fusion.2 = bf16[128,7168]{1,0:T(8,128)(2,1)} fusion(f32[2,128]{1,0:T(2,128)S(1)} %bitcast.61, bf16[1,7168,2]{1,2,0:T(2,128)(2,1)S(1)} %copy-done, bf16[1,128,7168]{2,1,0:T(8,128)(2,1)S(1)} %copy-done.1), kind=kOutput, calls=%fused_computation.5 | convolution fusion | flops 24772608 | bytes 3699712 | tf_op jit(solution)/shard_map/dot_general | solution.py:55
  120.9 3.8 %collective-permute-start = (bf16[128,7168]{1,0:T(8,128)(2,1)}, bf16[128,7168]{1,0:T(8,128)(2,1)S(1)}, u32[]{:S(2)}, u32[]{:S(2)}) collective-permute-start(bf16[128,7168]{1,0:T(8,128)(2,1)} %fusion.2), channel_id=1, source_target_pairs={{8,0},{16,8},{24,16},{9,1},{17,9},{25,17},{10,2},{18,10},{26,18},{... | collective-permute-start | bytes 5505032 | tf_op jit(solution)/shard_map/ppermute | solution.py:10
  124.7 5.2 %fusion.1 = bf16[1,256,7168]{1,2,0:T(8,128)(2,1)} fusion(bf16[8,32,7168]{2,1,0:T(8,128)(2,1)} %all-to-all-done.1, f32[8,32]{1,0:T(8,128)S(1)} %bitcast.59, bf16[1,1,8,32,256]{4,3,2,1,0:T(8,128)(2,1)S(1)} %copy-done.3), kind=kOutput, calls=%fused_computation.3 | convolution fusion | flops 946864128 | bytes 7472128 | tf_op jit(solution)/shard_map/sch,scd->hd/dot_general | solution.py:44
  129.9 5.9 %copy.13 = bf16[1,256,7168]{2,1,0:T(8,128)(2,1)} copy(bf16[1,256,7168]{1,2,0:T(8,128)(2,1)} %fusion.1) | data formatting | bytes 7340032
  135.8 11.1 %collective-permute-done = bf16[128,7168]{1,0:T(8,128)(2,1)S(1)} collective-permute-done((bf16[128,7168]{1,0:T(8,128)(2,1)}, bf16[128,7168]{1,0:T(8,128)(2,1)S(1)}, u32[]{:S(2)}, u32[]{:S(2)}) %collective-permute-start) | collective-permute-done | bytes 1835040 | tf_op jit(solution)/shard_map/ppermute | solution.py:10
  146.9 1.2 copy.17
  (4 shorter events, 0.0 us)
Async XLA Ops:
  0.6 117.2 %copy-start = (bf16[1,7168,2]{1,2,0:T(2,128)(2,1)S(1)}, bf16[1,7168,2]{1,2,0:T(2,128)(2,1)}, u32[]{:S(2)}) copy-start(bf16[1,7168,2]{1,2,0:T(2,128)(2,1)} %param.8) | copy-start | bytes 86020
  2.0 11.7 %all-to-all-start = ((bf16[8,1,32]{2,1,0:T(2,128)(2,1)}), bf16[8,1,32]{2,1,0:T(2,128)(2,1)S(1)}, u32[]{:S(2)}, u32[]{:S(2)}) async-start(bf16[8,1,32]{2,1,0:T(2,128)(2,1)} %copy.12), calls=%async_computation | async-start | bytes 8192 | tf_op jit(solution)/shard_map/all_to_all | solution.py:34
  16.0 86.2 %copy-start.3 = (bf16[1,1,8,32,256]{4,3,2,1,0:T(8,128)(2,1)S(1)}, bf16[1,1,8,32,256]{4,3,2,1,0:T(8,128)(2,1)}, u32[]{:S(2)}) copy-start(bf16[1,1,8,32,256]{4,3,2,1,0:T(8,128)(2,1)} %param.10) | copy-start | bytes 393220
  16.0 86.2 %all-to-all-start.1 = ((bf16[8,32,7168]{2,1,0:T(8,128)(2,1)}), bf16[8,32,7168]{2,1,0:T(8,128)(2,1)}, u32[]{:S(2)}, u32[]{:S(2)}) async-start(bf16[8,32,7168]{2,1,0:T(8,128)(2,1)} %bitcast.53), calls=%async_computation.1 | async-start | bytes 7340032 | tf_op jit(solution)/shard_map/all_to_all | solution.py:33
  102.2 15.5 %copy-start.2 = (s32[1,1,2,32]{3,2,1,0:T(2,128)S(1)}, s32[1,1,2,32]{3,2,1,0:T(2,128)}, u32[]{:S(2)}) copy-start(s32[1,1,2,32]{3,2,1,0:T(2,128)} %param.11) | copy-start | bytes 772
  102.2 15.7 %copy-start.1 = (bf16[1,128,7168]{2,1,0:T(8,128)(2,1)S(1)}, bf16[1,128,7168]{2,1,0:T(8,128)(2,1)}, u32[]{:S(2)}) copy-start(bf16[1,128,7168]{2,1,0:T(8,128)(2,1)} %param.7) | copy-start | bytes 5505028
  120.9 26.1 %collective-permute-start = (bf16[128,7168]{1,0:T(8,128)(2,1)}, bf16[128,7168]{1,0:T(8,128)(2,1)S(1)}, u32[]{:S(2)}, u32[]{:S(2)}) collective-permute-start(bf16[128,7168]{1,0:T(8,128)(2,1)} %fusion.2), channel_id=1, source_target_pairs={{8,0},{16,8},{24,16},{9,1},{17,9},{25,17},{10,2},{18,10},{26,18},{... | collective-permute-start | bytes 5505032 | tf_op jit(solution)/shard_map/ppermute | solution.py:10
where the time goes:
time: 149 us; the launch traced here: 148 us
  waiting for transfers between devices  91.7 us (62%)
  starting transfers between devices  15.7 us (11%)
  local copies, waits for them, and re-layouts  13.8 us (9%)
  matrix products  13.5 us (9%)
  blocking collectives  10.3 us (7%)
  other arithmetic  2.33 us (2%)
    all_to_all x1, waiting for transfers between devices, shards(): lax.all_to_all(sent, 'expert', split_axis=0, concat_axis=0, tiled=True)  80.6 us
    ppermute x1, waiting for transfers between devices, passed_along(): lax.ppermute(value, axis, [(source, source + steps) for source in range(i...  11.1 us
    all_to_all x1, blocking collectives, shards(): lax.all_to_all(partial_value, 'expert', split_axis=0, concat_axis=0, tile...  10.3 us
    unnamed x10, local copies, waits for them, and re-layouts  7.17 us
    all_to_all x1, starting transfers between devices, shards(): lax.all_to_all(gate_sent.astype(jnp.bfloat16), 'expert', split_axis=0, co...  6.35 us
    all_to_all x1, starting transfers between devices, shards(): lax.all_to_all(sent, 'expert', split_axis=0, concat_axis=0, tiled=True)  5.57 us
    dot_general x1, matrix products, shards(): jnp.einsum('sch,scd->hd', held, scaled, preferred_element_type=jnp.float32)  5.19 us
    dot_general x1, matrix products, shards(): jnp.einsum('scd,hd->sch', got_rows, w_block, preferred_element_type=jnp.f...  5.09 us
  transfers between devices with their start and end apart: 3, of which 2 were waited for; matrix products, arithmetic and copies ran while one was open for 11% of the time, Pallas kernels for 0%

commit v1 on v0

v1 whole, which is shorter than its diff:
```python
import functools

import jax
import jax.numpy as jnp
from jax import lax
from jax.experimental import pallas as pl
from jax.experimental.pallas import tpu as pltpu
from jax.sharding import PartitionSpec as P

MESH = pl.DeviceIdType.MESH
F32 = jnp.float32
BF16 = jnp.bfloat16
CHUNK = 512
LEAD = 2


def exchange(
    sizes,
    tok_ref, cnt_ref, gate_ref, held_ref, router_ref, grad_hbm, w_hbm,
    scaled_hbm, held_t_ref, hg_ref, next_hbm, rnext_hbm, logit_ref,
    gradv, wv, buf, outbuf, scaledv, proj, onehot, gsend, grecv, gcol,
    tsend, trecv, rsend, psend, precv,
    s_out, s_own, s_fwd, s_diag, s_gate, s_next, s_small, s_part,
    r_blk, r_gate, r_next, r_small, r_part, l_grad, l_w, l_scaled,
):
    sections, owners, experts, cap, chunks = sizes
    group = owners // experts
    width = gradv.shape[2]
    toks = gradv.shape[1]
    sec = lax.axis_index("section")
    me = lax.axis_index("expert")
    mine = me // group
    member = lax.rem(me, group)
    hi, lo = member // 2, lax.rem(member, 2)
    far_m = (1 - hi) * 2 + lo
    side_m = hi * 2 + (1 - lo)
    diag_m = (1 - hi) * 2 + (1 - lo)

    def at_expert(index):
        return {"section": sec, "expert": index}

    def at_previous(index):
        return {"section": sec - 1, "expert": index}

    def in_group(r, m):
        return lax.rem(mine + r, experts) * group + m

    def block(source, c):
        return buf.at[c, pl.ds(pl.multiple_of(source * cap, cap), cap)]

    def grad_load(c):
        return pltpu.make_async_copy(
            grad_hbm.at[:, pl.ds(pl.multiple_of(c * width, width), width)], gradv.at[c], l_grad.at[c])

    def w_load(c):
        return pltpu.make_async_copy(
            w_hbm.at[:, pl.ds(pl.multiple_of(c * width, width), width)], wv.at[c], l_w.at[c])

    def scaled_store(c):
        return pltpu.make_async_copy(scaledv.at[c], scaled_hbm.at[c], l_scaled.at[c])

    def send(src, dst, s_sem, r_sem, device):
        return pltpu.make_async_remote_copy(
            src_ref=src, dst_ref=dst, send_sem=s_sem, recv_sem=r_sem,
            device_id=device, device_id_type=MESH)

    def out_copy(r, c):
        return send(outbuf.at[r - 1, c], block(me, c), s_out.at[r - 1, c], r_blk.at[me, c],
                    at_expert(in_group(r, member)))

    def relay(source, c, s_sem, m):
        return send(block(source, c), block(source, c), s_sem, r_blk.at[source, c],
                    at_expert(in_group(0, m)))

    def own_copy(side, c):
        return relay(me, c, s_own.at[side, c], side_m if side else far_m)

    def fwd_copy(r, side, c):
        return relay(in_group(r, member), c, s_fwd.at[r - 1, side, c], side_m if side else far_m)

    def diag_by_far(r, c):
        return relay(in_group(r, far_m), c, s_diag.at[r, c], side_m)

    def diag_by_side(r, c):
        return relay(in_group(r, side_m), c, s_diag.at[r, c], far_m)

    def got(source, c):
        relay(source, c, s_own.at[0, c], far_m).wait_recv()

    def next_copy(c):
        return send(gradv.at[c], next_hbm.at[c], s_next.at[c], r_next.at[c], at_previous(me))

    def router_copy():
        return send(rsend, rnext_hbm, s_small.at[0], r_small.at[0], at_previous(me))

    def token_copy():
        return send(tsend, trecv, s_small.at[1], r_small.at[1], at_previous(me))

    def gate_copy(r, q):
        return send(gsend.at[r], grecv.at[me], s_gate.at[r, q], r_gate.at[me],
                    at_expert(in_group(r, lax.rem(member + q, group))))

    def part_copy(i):
        return send(psend.at[i], precv.at[me], s_part.at[i], r_part.at[me], at_previous(i))

    gate_pairs = [(r, q) for r in range(experts) for q in range(group) if r or q]

    barrier = pltpu.get_barrier_semaphore()
    for step in range(1, owners):
        pl.semaphore_signal(barrier, inc=1, device_id=at_expert(lax.rem(me + step, owners)),
                            device_id_type=MESH)

    @pl.when(sec < sections - 1)
    def _():
        for i in range(owners):
            pl.semaphore_signal(barrier, inc=1, device_id={"section": sec + 1, "expert": i},
                                device_id_type=MESH)

    def start_grad(c, carry):
        grad_load(c).start()
        return carry

    def start_w(c, carry):
        w_load(c).start()
        return carry

    lax.fori_loop(0, chunks, start_grad, 0)
    lax.fori_loop(0, chunks, start_w, 0)

    eye = lax.broadcasted_iota(jnp.int32, (cap, cap), 0) == lax.broadcasted_iota(jnp.int32, (cap, cap), 1)
    slot = lax.broadcasted_iota(jnp.int32, (1, cap), 1)

    def column(row):
        return jnp.sum(jnp.where(eye, row, 0.0), axis=1, keepdims=True)

    def row_of(col):
        return jnp.sum(jnp.where(eye, col, 0.0), axis=0, keepdims=True)

    places = lax.broadcasted_iota(jnp.int32, (cap, toks), 1).astype(F32)
    gsend[...] = jnp.zeros_like(gsend)
    tsend[...] = jnp.full(tsend.shape, -1, jnp.int32)
    for r in range(experts):
        e = lax.rem(mine + r, experts)
        live = slot < cnt_ref[e]
        tok = jnp.where(live, tok_ref[pl.ds(e, 1), :], -1)
        hit = jnp.where(column(tok.astype(F32)) == places, 1.0, 0.0)
        onehot[r * cap:(r + 1) * cap, :] = hit.astype(BF16)
        gsend[r, 0:1, 0:cap] = jnp.where(live, gate_ref[pl.ds(e, 1), :], 0.0)
    for e in range(experts):
        tsend[e:e + 1, 0:cap] = jnp.where(slot < cnt_ref[e], tok_ref[e:e + 1, :], -1)
    grecv[me] = gsend[0]
    rsend[...] = jnp.zeros_like(rsend)
    rsend[0:experts, :] = router_ref[...]

    def gather(c):
        grad_load(c).wait()
        rows = lax.dot_general(onehot[...], gradv[c], (((1,), (0,)), ((), ())),
                               preferred_element_type=F32).astype(BF16)
        buf[c, pl.ds(pl.multiple_of(me * cap, cap), cap), :] = rows[:cap]
        for r in range(1, experts):
            outbuf[r - 1, c] = rows[r * cap:(r + 1) * cap]

    gather(0)
    pl.semaphore_wait(barrier, (owners - 1) + jnp.where(sec > 0, owners, 0))

    def step(t, carry):
        @pl.when(t < chunks)
        def _():
            for r in range(1, experts):
                out_copy(r, t).start()
            own_copy(0, t).start()
            own_copy(1, t).start()

            @pl.when(t + 1 < chunks)
            def _():
                gather(t + 1)

            @pl.when(sec > 0)
            def _():
                next_copy(t).start()

        @pl.when(t == 0)
        def _():
            for r, q in gate_pairs:
                gate_copy(r, q).start()

            @pl.when(sec > 0)
            def _():
                router_copy().start()
                token_copy().start()

        c1 = t - LEAD

        @pl.when((c1 >= 0) & (c1 < chunks))
        def _():
            for r in range(1, experts):
                got(in_group(r, member), c1)
                fwd_copy(r, 0, c1).start()
                fwd_copy(r, 1, c1).start()

        c2 = t - 2 * LEAD

        @pl.when((c2 >= 0) & (c2 < chunks))
        def _():
            for r in range(experts):
                got(in_group(r, far_m), c2)
                got(in_group(r, side_m), c2)
                side_first = lax.rem(c2 + 2 * r, 4) == 1

                @pl.when(side_first)
                def _():
                    diag_by_side(r, c2).start()

                @pl.when(jnp.logical_not(side_first))
                def _():
                    diag_by_far(r, c2).start()

        c3 = t - 3 * LEAD

        @pl.when(c3 == 0)
        def _():
            for i in range(1, owners):
                other = lax.rem(me + i, owners)
                send(gsend.at[0], grecv.at[other], s_gate.at[0, 1], r_gate.at[other],
                     at_expert(other)).wait_recv()
            for i in range(owners):
                gcol[i * cap:(i + 1) * cap, :] = jnp.broadcast_to(
                    column(grecv[i, 0:1, 0:cap]), (cap, gcol.shape[1]))
            held_t_ref[...] = held_ref[...].astype(F32).T.astype(BF16)
            proj[...] = jnp.zeros_like(proj)

        @pl.when(c3 >= 0)
        def _():
            for r in range(experts):
                got(in_group(r, diag_m), c3)
            w_load(c3).wait()
            proj[...] += lax.dot_general(buf[c3], wv[c3], (((1,), (1,)), ((), ())),
                                         preferred_element_type=F32)
            for p in range(0, width, 128):
                scaledv[c3, :, p:p + 128] = (gcol[...] * buf[c3, :, p:p + 128].astype(F32)).astype(BF16)
            scaled_store(c3).start()

        return carry

    lax.fori_loop(0, chunks + 3 * LEAD, step, 0)

    partial = jnp.sum(held_ref[...].astype(F32) * proj[...], axis=1, keepdims=True)
    psend[...] = jnp.zeros_like(psend)
    for i in range(owners):
        psend[i, 0:1, 0:cap] = row_of(partial[i * cap:(i + 1) * cap])

    @pl.when(sec > 0)
    def _():
        for i in range(owners):
            part_copy(i).start()

    hg_ref[...] = (gcol[:, 0:1] * proj[...]).astype(BF16)

    def drain(c, carry):
        for r in range(1, experts):
            out_copy(r, c).wait_send()
            fwd_copy(r, 0, c).wait_send()
            fwd_copy(r, 1, c).wait_send()
        own_copy(0, c).wait_send()
        own_copy(1, c).wait_send()
        for r in range(experts):
            diag_by_far(r, c).wait_send()

        @pl.when(sec > 0)
        def _():
            next_copy(c).wait_send()

        @pl.when(sec < sections - 1)
        def _():
            next_copy(c).wait_recv()

        scaled_store(c).wait()
        return carry

    lax.fori_loop(0, chunks, drain, 0)
    for r, q in gate_pairs:
        gate_copy(r, q).wait_send()

    logit_ref[...] = jnp.zeros_like(logit_ref)

    @pl.when(sec < sections - 1)
    def _():
        router_copy().wait_recv()
        token_copy().wait_recv()
        for j in range(owners):
            send(psend.at[j], precv.at[j], s_part.at[j], r_part.at[j], at_expert(j)).wait_recv()
        lane = lax.broadcasted_iota(jnp.int32, logit_ref.shape, 1)
        where_tok = lax.broadcasted_iota(jnp.int32, (toks, cap), 0)
        total = jnp.zeros(logit_ref.shape, F32)
        for e in range(experts):
            gate_grad = precv[e * group, 0:1, 0:cap]
            for q in range(1, group):
                gate_grad = gate_grad + precv[e * group + q, 0:1, 0:cap]
            match = where_tok == trecv[e:e + 1, 0:cap]
            col = jnp.sum(jnp.where(match, gate_grad, 0.0), axis=1, keepdims=True)
            total = jnp.where(lane == e, col, total)
        logit_ref[...] = total

    @pl.when(sec > 0)
    def _():
        router_copy().wait_send()
        token_copy().wait_send()
        for i in range(owners):
            part_copy(i).wait_send()


def finish(sections, experts, held_t_ref, scaled_ref, logit_ref, next_ref, router_ref, down_ref, passed_ref):
    down_ref[...] = jnp.dot(held_t_ref[...], scaled_ref[0], preferred_element_type=F32).astype(BF16)
    total = next_ref[0].astype(F32)
    for e in range(experts):
        total = total + logit_ref[:, e:e + 1] * router_ref[e:e + 1, :].astype(F32)
    last = lax.axis_index("section") == sections - 1
    passed_ref[...] = jnp.where(last, 0.0, total).astype(BF16)


def shards(out_grad, router_weight, down_weight, hidden_saved, slot_token, slot_count, slot_gate):
    sections, owners = lax.axis_size("section"), lax.axis_size("expert")
    grad, w_block = out_grad[0], down_weight[0]
    toks, width = grad.shape
    hid = w_block.shape[0]
    experts, cap = slot_token.shape[2:]
    group = owners // experts
    assert group == 4 and width % CHUNK == 0
    chunks = width // CHUNK
    slots = owners * cap
    pad_e = -(-experts // 8) * 8
    pad_r = -(-experts // 16) * 16
    held = hidden_saved.reshape(slots, hid)
    vmem = pl.BlockSpec(memory_space=pltpu.VMEM)
    smem = pl.BlockSpec(memory_space=pltpu.SMEM)
    anyw = pl.BlockSpec(memory_space=pl.ANY)
    dma = pltpu.SemaphoreType.DMA
    shape = jax.ShapeDtypeStruct
    scratch = [
        pltpu.VMEM((chunks, toks, CHUNK), BF16),
        pltpu.VMEM((chunks, hid, CHUNK), BF16),
        pltpu.VMEM((chunks, slots, CHUNK), BF16),
        pltpu.VMEM((experts - 1, chunks, cap, CHUNK), BF16),
        pltpu.VMEM((chunks, slots, CHUNK), BF16),
        pltpu.VMEM((slots, hid), F32),
        pltpu.VMEM((experts * cap, toks), BF16),
        pltpu.VMEM((experts, 8, 128), F32),
        pltpu.VMEM((owners, 8, 128), F32),
        pltpu.VMEM((slots, 128), F32),
        pltpu.VMEM((pad_e, 128), jnp.int32),
        pltpu.VMEM((pad_e, 128), jnp.int32),
        pltpu.VMEM((pad_r, width), BF16),
        pltpu.VMEM((owners, 8, 128), F32),
        pltpu.VMEM((owners, 8, 128), F32),
    ]
    used = sum(2 * s.shape[0] * functools.reduce(lambda a, b: a * b, s.shape[1:]) * (s.dtype.itemsize // 2)
               for s in scratch)
    scratch += [
        dma((experts - 1, chunks)), dma((2, chunks)), dma((experts - 1, 2, chunks)), dma((experts, chunks)),
        dma((experts, group)), dma((chunks,)), dma((2,)), dma((owners,)),
        dma((owners, chunks)), dma((owners,)), dma((chunks,)), dma((2,)), dma((owners,)),
        dma((chunks,)), dma((chunks,)), dma((chunks,)),
    ]
    scaled, held_t, hidden_grad, following, router_next, logit = pl.pallas_call(
        functools.partial(exchange, (sections, owners, experts, cap, chunks)),
        out_shape=(
            shape((chunks, slots, CHUNK), BF16),
            shape((hid, slots), BF16),
            shape((slots, hid), BF16),
            shape((chunks, toks, CHUNK), BF16),
            shape((pad_r, width), BF16),
            shape((toks, 128), F32),
        ),
        in_specs=[vmem, smem, vmem, vmem, vmem, anyw, anyw],
        out_specs=(anyw, vmem, vmem, anyw, anyw, vmem),
        scratch_shapes=scratch,
        compiler_params=pltpu.CompilerParams(
            collective_id=0, has_side_effects=True, vmem_limit_bytes=used + 12 * 2**20),
        cost_estimate=pl.CostEstimate(
            flops=2 * slots * hid * width, bytes_accessed=2 * width * (2 * toks + hid + slots),
            transcendentals=0),
    )(slot_token[0, 0], slot_count[0, 0], slot_gate[0, 0], held, router_weight[0].T, grad, w_block)

    down_grad, passed = pl.pallas_call(
        functools.partial(finish, sections, experts),
        grid=(chunks,),
        out_shape=(shape((hid, width), BF16), shape((toks, width), BF16)),
        in_specs=[
            pl.BlockSpec((hid, slots), lambda k: (0, 0)),
            pl.BlockSpec((1, slots, CHUNK), lambda k: (k, 0, 0)),
            pl.BlockSpec((toks, 128), lambda k: (0, 0)),
            pl.BlockSpec((1, toks, CHUNK), lambda k: (k, 0, 0)),
            pl.BlockSpec((pad_r, CHUNK), lambda k: (0, k)),
        ],
        out_specs=(
            pl.BlockSpec((hid, CHUNK), lambda k: (0, k)),
            pl.BlockSpec((toks, CHUNK), lambda k: (0, k)),
        ),
        compiler_params=pltpu.CompilerParams(vmem_limit_bytes=24 * 2**20),
        cost_estimate=pl.CostEstimate(
            flops=2 * slots * hid * width, bytes_accessed=2 * width * (2 * toks + hid + slots),
            transcendentals=0),
    )(held_t, scaled, logit, following, router_next)
    return down_grad[None], hidden_grad.reshape(hidden_saved.shape), passed[None]


def solution(mesh):
    return jax.shard_map(
        shards,
        mesh=mesh,
        in_specs=(
            P("section", "expert", None),
            P("section", None, None),
            P("section", "expert", None),
            P("section", "expert", None, None, None),
            P("section", "expert", None, None),
            P("section", "expert", None),
            P("section", "expert", None, None),
        ),
        out_specs=(
            P("section", "expert", None),
            P("section", "expert", None, None, None),
            P("section", "expert", None),
        ),
        check_vma=False,
    )
```

time: 149 us -> 68.9 us (0.46)
  waiting for transfers between devices: 91.7 us -> 0 us
  Pallas kernels: 0 us -> 60 us
  starting transfers between devices: 15.7 us -> 0 us
  matrix products: 13.5 us -> 0 us
  blocking collectives: 10.3 us -> 0 us
  local copies, waits for them, and re-layouts: 13.8 us -> 7.85 us
  other arithmetic: 2.33 us -> 0 us
    all_to_all x2 -> x0, waiting for transfers between devices: 80.6 us -> none  [the longest x1 80.6 us: shards(): lax.all_to_all(sent, 'expert', split_axis=0, concat_axis=0, tiled=True)]
    pallas_call x0 -> x2, Pallas kernels: none -> 60 us  [the longest x1 53.2 us: shards(): pl.pallas_call(functools.partial(exchange, (sections, owners, experts, ca...]
    dot_general x4 -> x0, matrix products: 13.5 us -> none  [the longest x1 5.19 us: shards(): jnp.einsum('sch,scd->hd', held, scaled, preferred_element_type=jnp.float32)]
    all_to_all x2 -> x0, starting transfers between devices: 11.9 us -> none  [the longest x1 6.35 us: shards(): lax.all_to_all(gate_sent.astype(jnp.bfloat16), 'expert', split_axis=0, co...]
    ppermute x1 -> x0, waiting for transfers between devices: 11.1 us -> none  [passed_along(): lax.ppermute(value, axis, [(source, source + steps) for source in range(i...]
    all_to_all x1 -> x0, blocking collectives: 10.3 us -> none  [shards(): lax.all_to_all(partial_value, 'expert', split_axis=0, concat_axis=0, tile...]
    ppermute x1 -> x0, starting transfers between devices: 3.82 us -> none  [passed_along(): lax.ppermute(value, axis, [(source, source + steps) for source in range(i...]
    gather x1 -> x0, local copies, waits for them, and re-layouts: 3.69 us -> none  [shards(): rows = jnp.where(live[..., None], grad[tokens], jnp.zeros((), grad.dtype))]
  transfers between devices with their start and end apart: 3 -> 0, of which waited for: 2 -> 0; matrix products, arithmetic and copies ran while one was open for 11% -> 0% of each run, Pallas kernels for 0% -> 0%
where the time goes in v1:
time: 68.9 us; the launch traced here: 68.5 us
  Pallas kernels  60 us (87%)
  local copies, waits for them, and re-layouts  7.85 us (11%)
    pallas_call x1, Pallas kernels, shards(): pl.pallas_call(functools.partial(exchange, (sections, owners, experts, ca...  53.2 us
    unnamed x15, local copies, waits for them, and re-layouts  7.85 us
    pallas_call x1, Pallas kernels, shards(): pl.pallas_call(functools.partial(finish, sections, experts), grid=(chunks...  6.85 us

profile of v1, /device:TPU:1, one launch (start us, length us, event | category | flops | bytes accessed | tf_op | source)
XLA Modules:
  0.0 68.5 jit_solution(8450187255256446310)
XLA Ops:
  0.6 0.0 copy-start
  0.6 2.0 %copy-done = bf16[1,256,7168]{2,1,0:T(8,128)(2,1)S(1)} copy-done((bf16[1,256,7168]{2,1,0:T(8,128)(2,1)S(1)}, bf16[1,256,7168]{2,1,0:T(8,128)(2,1)}, u32[]{:S(2)}) %copy-start) | copy-done | bytes 3670040
  2.7 0.0 copy-start.1
  2.7 1.5 %copy-done.1 = bf16[1,128,7168]{2,1,0:T(8,128)(2,1)S(1)} copy-done((bf16[1,128,7168]{2,1,0:T(8,128)(2,1)S(1)}, bf16[1,128,7168]{2,1,0:T(8,128)(2,1)}, u32[]{:S(2)}) %copy-start.1) | copy-done | bytes 1835032
  4.2 0.0 copy-start.2
  4.2 0.9 %copy-done.2 = bf16[1,1,8,32,256]{4,3,2,1,0:T(8,128)(2,1)S(1)} copy-done((bf16[1,1,8,32,256]{4,3,2,1,0:T(8,128)(2,1)S(1)}, bf16[1,1,8,32,256]{4,3,2,1,0:T(8,128)(2,1)}, u32[]{:S(2)}) %copy-start.2) | copy-done | bytes 131096
  5.1 0.0 copy-start.3
  5.1 0.7 %copy-done.3 = bf16[1,7168,2]{1,2,0:T(2,128)(2,1)S(1)} copy-done((bf16[1,7168,2]{1,2,0:T(2,128)(2,1)S(1)}, bf16[1,7168,2]{1,2,0:T(2,128)(2,1)}, u32[]{:S(2)}) %copy-start.3) | copy-done | bytes 28696
  5.8 0.0 copy-start.4
  5.8 0.7 copy-done.4
  6.5 0.0 copy-start.5
  6.5 0.7 copy-done.5
  7.2 0.0 copy-start.6
  7.2 0.7 copy-done.6
  7.8 53.2 %shard_map.94 = (bf16[14,256,512]{2,1,0:T(8,128)(2,1)S(1)}, bf16[256,256]{1,0:T(8,128)(2,1)S(1)}, bf16[256,256]{1,0:T(8,128)(2,1)S(1)}, bf16[14,128,512]{2,1,0:T...) custom-call(s32[2,32]{1,0:T(2,128)S(1)} %bitcast.17, s32[2]{0:T(128)S(1)} %bitcast.19, ...), custom_call_target="tpu_custom_call" | custom-call | flops 939524096 | bytes 11010048 | tf_op jit(solution)/shard_map/pallas_call | solution.py:364
  61.0 6.9 %shard_map.95 = (bf16[256,7168]{1,0:T(8,128)(2,1)}, bf16[128,7168]{1,0:T(8,128)(2,1)}) custom-call(bf16[256,256]{1,0:T(8,128)(2,1)S(1)} %get-tuple-element.11.held_t_ref, bf16[14,256,512]{2,1,0:T(8,128)(2,1)S(1)} %get-tuple-element.12.scaled_ref, f32[128,128]{1,0:T(8,128)S(1)} %get-tuple-element.13.logit_ref, ...), custom_call_target="tpu_custom_call" | custom-call | flops 939524096 | bytes 11010048 | tf_op jit(solution)/shard_map/pallas_call | solution.py:384
  67.9 0.7 copy.11
Async XLA Ops:
  0.6 2.0 %copy-start = (bf16[1,256,7168]{2,1,0:T(8,128)(2,1)S(1)}, bf16[1,256,7168]{2,1,0:T(8,128)(2,1)}, u32[]{:S(2)}) copy-start(bf16[1,256,7168]{2,1,0:T(8,128)(2,1)} %param.9) | copy-start | bytes 11010052
  2.7 1.5 %copy-start.1 = (bf16[1,128,7168]{2,1,0:T(8,128)(2,1)S(1)}, bf16[1,128,7168]{2,1,0:T(8,128)(2,1)}, u32[]{:S(2)}) copy-start(bf16[1,128,7168]{2,1,0:T(8,128)(2,1)} %param.7) | copy-start | bytes 5505028
  4.2 0.9 %copy-start.2 = (bf16[1,1,8,32,256]{4,3,2,1,0:T(8,128)(2,1)S(1)}, bf16[1,1,8,32,256]{4,3,2,1,0:T(8,128)(2,1)}, u32[]{:S(2)}) copy-start(bf16[1,1,8,32,256]{4,3,2,1,0:T(8,128)(2,1)} %param.10) | copy-start | bytes 393220
  5.1 0.7 %copy-start.3 = (bf16[1,7168,2]{1,2,0:T(2,128)(2,1)S(1)}, bf16[1,7168,2]{1,2,0:T(2,128)(2,1)}, u32[]{:S(2)}) copy-start(bf16[1,7168,2]{1,2,0:T(2,128)(2,1)} %param.8) | copy-start | bytes 86020
  5.8 0.7 copy-start.4
  6.5 0.7 copy-start.5
  7.2 0.7 copy-start.6

commit v2 on v1

--- a/solution.py
+++ b/solution.py
@@ -16,12 +16,13 @@
 
 def exchange(
     sizes,
-    tok_ref, cnt_ref, gate_ref, held_ref, router_ref, grad_hbm, w_hbm,
+    tok_hbm, cnt_hbm, gate_hbm, held_hbm, router_hbm, grad_hbm, w_hbm,
     scaled_hbm, held_t_ref, hg_ref, next_hbm, rnext_hbm, logit_ref,
+    tok_ref, cnt_ref, gate_ref, held_ref, router_ref,
     gradv, wv, buf, outbuf, scaledv, proj, onehot, gsend, grecv, gcol,
     tsend, trecv, rsend, psend, precv,
     s_out, s_own, s_fwd, s_diag, s_gate, s_next, s_small, s_part,
-    r_blk, r_gate, r_next, r_small, r_part, l_grad, l_w, l_scaled,
+    r_blk, r_gate, r_next, r_small, r_part, l_grad, l_w, l_scaled, l_in,
 ):
     sections, owners, experts, cap, chunks = sizes
     group = owners // experts
@@ -105,6 +106,18 @@
 
     gate_pairs = [(r, q) for r in range(experts) for q in range(group) if r or q]
 
+    loads = [
+        pltpu.make_async_copy(src, dst, l_in.at[i])
+        for i, (src, dst) in enumerate((
+            (tok_hbm, tok_ref), (cnt_hbm, cnt_ref), (gate_hbm, gate_ref),
+            (router_hbm, router_ref), (held_hbm, held_ref)))
+    ]
+    for load in loads[:3]:
+        load.start()
+    grad_load(0).start()
+    for load in loads[3:]:
+        load.start()
+
     barrier = pltpu.get_barrier_semaphore()
     for step in range(1, owners):
         pl.semaphore_signal(barrier, inc=1, device_id=at_expert(lax.rem(me + step, owners)),
@@ -124,11 +137,18 @@
         w_load(c).start()
         return carry
 
-    lax.fori_loop(0, chunks, start_grad, 0)
+    lax.fori_loop(1, chunks, start_grad, 0)
     lax.fori_loop(0, chunks, start_w, 0)
 
     eye = lax.broadcasted_iota(jnp.int32, (cap, cap), 0) == lax.broadcasted_iota(jnp.int32, (cap, cap), 1)
     slot = lax.broadcasted_iota(jnp.int32, (1, cap), 1)
+    for load in loads[:3]:
+        load.wait()
+    counts = cnt_ref[...].astype(F32)
+    entry = lax.broadcasted_iota(jnp.int32, counts.shape, 1)
+
+    def alive(e):
+        return slot.astype(F32) < jnp.sum(jnp.where(entry == e, counts, 0.0), axis=1, keepdims=True)
 
     def column(row):
         return jnp.sum(jnp.where(eye, row, 0.0), axis=1, keepdims=True)
@@ -141,16 +161,14 @@
     tsend[...] = jnp.full(tsend.shape, -1, jnp.int32)
     for r in range(experts):
         e = lax.rem(mine + r, experts)
-        live = slot < cnt_ref[e]
+        live = alive(e)
         tok = jnp.where(live, tok_ref[pl.ds(e, 1), :], -1)
         hit = jnp.where(column(tok.astype(F32)) == places, 1.0, 0.0)
         onehot[r * cap:(r + 1) * cap, :] = hit.astype(BF16)
         gsend[r, 0:1, 0:cap] = jnp.where(live, gate_ref[pl.ds(e, 1), :], 0.0)
     for e in range(experts):
-        tsend[e:e + 1, 0:cap] = jnp.where(slot < cnt_ref[e], tok_ref[e:e + 1, :], -1)
+        tsend[e:e + 1, 0:cap] = jnp.where(alive(e), tok_ref[e:e + 1, :], -1)
     grecv[me] = gsend[0]
-    rsend[...] = jnp.zeros_like(rsend)
-    rsend[0:experts, :] = router_ref[...]
 
     def gather(c):
         grad_load(c).wait()
@@ -161,7 +179,28 @@
             outbuf[r - 1, c] = rows[r * cap:(r + 1) * cap]
 
     gather(0)
+    rsend[...] = jnp.zeros_like(rsend)
+    loads[3].wait()
+    rsend[0:experts, :] = router_ref[...]
     pl.semaphore_wait(barrier, (owners - 1) + jnp.where(sec > 0, owners, 0))
+
+    def drain(c):
+        for r in range(1, experts):
+            out_copy(r, c).wait_send()
+            fwd_copy(r, 0, c).wait_send()
+            fwd_copy(r, 1, c).wait_send()
+        own_copy(0, c).wait_send()
+        own_copy(1, c).wait_send()
+        for r in range(experts):
+            diag_by_far(r, c).wait_send()
+
+        @pl.when(sec > 0)
+        def _():
+            next_copy(c).wait_send()
+
+        @pl.when(sec < sections - 1)
+        def _():
+            next_copy(c).wait_recv()
 
     def step(t, carry):
         @pl.when(t < chunks)
@@ -226,6 +265,7 @@
             for i in range(owners):
                 gcol[i * cap:(i + 1) * cap, :] = jnp.broadcast_to(
                     column(grecv[i, 0:1, 0:cap]), (cap, gcol.shape[1]))
+            loads[4].wait()
             held_t_ref[...] = held_ref[...].astype(F32).T.astype(BF16)
             proj[...] = jnp.zeros_like(proj)
 
@@ -239,6 +279,11 @@
             for p in range(0, width, 128):
                 scaledv[c3, :, p:p + 128] = (gcol[...] * buf[c3, :, p:p + 128].astype(F32)).astype(BF16)
             scaled_store(c3).start()
+            drain(c3)
+
+            @pl.when(c3 > 0)
+            def _():
+                scaled_store(c3 - 1).wait()
 
         return carry
 
@@ -256,28 +301,7 @@
 
     hg_ref[...] = (gcol[:, 0:1] * proj[...]).astype(BF16)
 
-    def drain(c, carry):
-        for r in range(1, experts):
-            out_copy(r, c).wait_send()
-            fwd_copy(r, 0, c).wait_send()
-            fwd_copy(r, 1, c).wait_send()
-        own_copy(0, c).wait_send()
-        own_copy(1, c).wait_send()
-        for r in range(experts):
-            diag_by_far(r, c).wait_send()
-
-        @pl.when(sec > 0)
-        def _():
-            next_copy(c).wait_send()
-
-        @pl.when(sec < sections - 1)
-        def _():
-            next_copy(c).wait_recv()
-
-        scaled_store(c).wait()
-        return carry
-
-    lax.fori_loop(0, chunks, drain, 0)
+    scaled_store(chunks - 1).wait()
     for r, q in gate_pairs:
         gate_copy(r, q).wait_send()
 
@@ -309,13 +333,23 @@
             part_copy(i).wait_send()
 
 
-def finish(sections, experts, held_t_ref, scaled_ref, logit_ref, next_ref, router_ref, down_ref, passed_ref):
-    down_ref[...] = jnp.dot(held_t_ref[...], scaled_ref[0], preferred_element_type=F32).astype(BF16)
-    total = next_ref[0].astype(F32)
-    for e in range(experts):
-        total = total + logit_ref[:, e:e + 1] * router_ref[e:e + 1, :].astype(F32)
+def finish(
+    sections, experts, held_t_ref, hg_ref, scaled_ref, logit_ref, next_ref, router_ref,
+    down_ref, hidden_ref, passed_ref,
+):
+    @pl.when(pl.program_id(0) == 0)
+    def _():
+        hidden_ref[...] = hg_ref[...]
+
     last = lax.axis_index("section") == sections - 1
-    passed_ref[...] = jnp.where(last, 0.0, total).astype(BF16)
+    for c in range(scaled_ref.shape[0]):
+        cols = slice(c * CHUNK, (c + 1) * CHUNK)
+        down_ref[:, cols] = jnp.dot(
+            held_t_ref[...], scaled_ref[c], preferred_element_type=F32).astype(BF16)
+        total = next_ref[c].astype(F32)
+        for e in range(experts):
+            total = total + logit_ref[:, e:e + 1] * router_ref[e:e + 1, cols].astype(F32)
+        passed_ref[:, cols] = jnp.where(last, 0.0, total).astype(BF16)
 
 
 def shards(out_grad, router_weight, down_weight, hidden_saved, slot_token, slot_count, slot_gate):
@@ -332,11 +366,16 @@
     pad_r = -(-experts // 16) * 16
     held = hidden_saved.reshape(slots, hid)
     vmem = pl.BlockSpec(memory_space=pltpu.VMEM)
-    smem = pl.BlockSpec(memory_space=pltpu.SMEM)
+    hbm = pl.BlockSpec(memory_space=pltpu.HBM)
     anyw = pl.BlockSpec(memory_space=pl.ANY)
     dma = pltpu.SemaphoreType.DMA
     shape = jax.ShapeDtypeStruct
     scratch = [
+        pltpu.VMEM((experts, cap), jnp.int32),
+        pltpu.VMEM((1, experts), jnp.int32),
+        pltpu.VMEM((experts, cap), F32),
+        pltpu.VMEM((slots, hid), BF16),
+        pltpu.VMEM((experts, width), BF16),
         pltpu.VMEM((chunks, toks, CHUNK), BF16),
         pltpu.VMEM((chunks, hid, CHUNK), BF16),
         pltpu.VMEM((chunks, slots, CHUNK), BF16),
@@ -353,13 +392,11 @@
         pltpu.VMEM((owners, 8, 128), F32),
         pltpu.VMEM((owners, 8, 128), F32),
     ]
-    used = sum(2 * s.shape[0] * functools.reduce(lambda a, b: a * b, s.shape[1:]) * (s.dtype.itemsize // 2)
-               for s in scratch)
     scratch += [
         dma((experts - 1, chunks)), dma((2, chunks)), dma((experts - 1, 2, chunks)), dma((experts, chunks)),
         dma((experts, group)), dma((chunks,)), dma((2,)), dma((owners,)),
         dma((owners, chunks)), dma((owners,)), dma((chunks,)), dma((2,)), dma((owners,)),
-        dma((chunks,)), dma((chunks,)), dma((chunks,)),
+        dma((chunks,)), dma((chunks,)), dma((chunks,)), dma((5,)),
     ]
     scaled, held_t, hidden_grad, following, router_next, logit = pl.pallas_call(
         functools.partial(exchange, (sections, owners, experts, cap, chunks)),
@@ -371,37 +408,40 @@
             shape((pad_r, width), BF16),
             shape((toks, 128), F32),
         ),
-        in_specs=[vmem, smem, vmem, vmem, vmem, anyw, anyw],
+        in_specs=[hbm] * 7,
         out_specs=(anyw, vmem, vmem, anyw, anyw, vmem),
         scratch_shapes=scratch,
         compiler_params=pltpu.CompilerParams(
-            collective_id=0, has_side_effects=True, vmem_limit_bytes=used + 12 * 2**20),
+            collective_id=0, has_side_effects=True, vmem_limit_bytes=64 * 2**20),
         cost_estimate=pl.CostEstimate(
             flops=2 * slots * hid * width, bytes_accessed=2 * width * (2 * toks + hid + slots),
             transcendentals=0),
-    )(slot_token[0, 0], slot_count[0, 0], slot_gate[0, 0], held, router_weight[0].T, grad, w_block)
-
-    down_grad, passed = pl.pallas_call(
+    )(slot_token[0, 0], slot_count[0], slot_gate[0, 0], held, router_weight[0].T, grad, w_block)
+
+    per = 2 if chunks % 2 == 0 else 1
+    down_grad, hidden, passed = pl.pallas_call(
         functools.partial(finish, sections, experts),
-        grid=(chunks,),
-        out_shape=(shape((hid, width), BF16), shape((toks, width), BF16)),
+        grid=(chunks // per,),
+        out_shape=(shape((hid, width), BF16), shape((slots, hid), BF16), shape((toks, width), BF16)),
         in_specs=[
             pl.BlockSpec((hid, slots), lambda k: (0, 0)),
-            pl.BlockSpec((1, slots, CHUNK), lambda k: (k, 0, 0)),
+            pl.BlockSpec((slots, hid), lambda k: (0, 0)),
+            pl.BlockSpec((per, slots, CHUNK), lambda k: (k, 0, 0)),
             pl.BlockSpec((toks, 128), lambda k: (0, 0)),
-            pl.BlockSpec((1, toks, CHUNK), lambda k: (k, 0, 0)),
-            pl.BlockSpec((pad_r, CHUNK), lambda k: (0, k)),
+            pl.BlockSpec((per, toks, CHUNK), lambda k: (k, 0, 0)),
+            pl.BlockSpec((pad_r, per * CHUNK), lambda k: (0, k)),
         ],
         out_specs=(
-            pl.BlockSpec((hid, CHUNK), lambda k: (0, k)),
-            pl.BlockSpec((toks, CHUNK), lambda k: (0, k)),
+            pl.BlockSpec((hid, per * CHUNK), lambda k: (0, k)),
+            pl.BlockSpec((slots, hid), lambda k: (0, 0)),
+            pl.BlockSpec((toks, per * CHUNK), lambda k: (0, k)),
         ),
-        compiler_params=pltpu.CompilerParams(vmem_limit_bytes=24 * 2**20),
+        compiler_params=pltpu.CompilerParams(vmem_limit_bytes=64 * 2**20),
         cost_estimate=pl.CostEstimate(
             flops=2 * slots * hid * width, bytes_accessed=2 * width * (2 * toks + hid + slots),
             transcendentals=0),
-    )(held_t, scaled, logit, following, router_next)
-    return down_grad[None], hidden_grad.reshape(hidden_saved.shape), passed[None]
+    )(held_t, hidden_grad, scaled, logit, following, router_next)
+    return down_grad[None], hidden.reshape(hidden_saved.shape), passed[None]
 
 
 def solution(mesh):

time: 68.9 us -> 62.8 us (0.911)
  local copies, waits for them, and re-layouts: 7.85 us -> 0 us
  Pallas kernels: 60 us -> 61.9 us
    unnamed x15 -> x0, local copies, waits for them, and re-layouts: 7.85 us -> none
    pallas_call x1, Pallas kernels: 6.85 us -> 8.51 us  [shards(): pl.pallas_call(functools.partial(finish, sections, experts), grid=(chunks...]
where the time goes in v2:
time: 62.8 us; the launch traced here: 62.5 us
  Pallas kernels  61.9 us (99%)
  between operations  0.64 us (1%)
    pallas_call x1, Pallas kernels, shards(): pl.pallas_call(functools.partial(exchange, (sections, owners, experts, ca...  53.3 us
    pallas_call x1, Pallas kernels, shards(): pl.pallas_call(functools.partial(finish, sections, experts), grid=(chunks...  8.51 us

profile of v2, /device:TPU:1, one launch (start us, length us, event | category | flops | bytes accessed | tf_op | source)
XLA Modules:
  0.0 62.5 jit_solution(16391447192636898760)
XLA Ops:
  0.6 53.3 %shard_map.94 = (bf16[14,256,512]{2,1,0:T(8,128)(2,1)}, bf16[256,256]{1,0:T(8,128)(2,1)}, bf16[256,256]{1,0:T(8,128)(2,1)}, bf16[14,128,512]{2,1,0:T(8,128)(2,1)...) custom-call(s32[2,32]{1,0:T(2,128)} %bitcast.16, s32[1,2]{1,0:T(1,128)} %bitcast.18, f32[2,32]{1,0:T(2,128)} %bitcast.17, ...), custom_call_target="tpu_custom_call" | custom-call | flops 939524096 | bytes 11010048 | tf_op jit(solution)/shard_map/pallas_call | solution.py:401
  54.0 8.5 %shard_map.95 = (bf16[256,7168]{1,0:T(8,128)(2,1)}, bf16[256,256]{1,0:T(8,128)(2,1)}, bf16[128,7168]{1,0:T(8,128)(2,1)}) custom-call(bf16[256,256]{1,0:T(8,128)(2,1)} %get-tuple-element.12.held_t_ref, bf16[256,256]{1,0:T(8,128)(2,1)} %get-tuple-element.13.hg_ref, bf16[14,256,512]{2,1,0:T(8,128)(2,1)} %get-tuple-element.14.scaled_ref, ...), custom_call_target="tpu_custom_call" | custom-call | flops 939524096 | bytes 11010048 | tf_op jit(solution)/shard_map/pallas_call | solution.py:422

commit v3 on v2

--- a/solution.py
+++ b/solution.py
@@ -17,12 +17,12 @@
 def exchange(
     sizes,
     tok_hbm, cnt_hbm, gate_hbm, held_hbm, router_hbm, grad_hbm, w_hbm,
-    scaled_hbm, held_t_ref, hg_ref, next_hbm, rnext_hbm, logit_ref,
+    down_hbm, hg_hbm, next_hbm, rnext_hbm, logit_ref,
     tok_ref, cnt_ref, gate_ref, held_ref, router_ref,
-    gradv, wv, buf, outbuf, scaledv, proj, onehot, gsend, grecv, gcol,
+    gradv, wv, buf, outbuf, downv, hgv, held_t, proj, onehot, gsend, grecv, gcol,
     tsend, trecv, rsend, psend, precv,
     s_out, s_own, s_fwd, s_diag, s_gate, s_next, s_small, s_part,
-    r_blk, r_gate, r_next, r_small, r_part, l_grad, l_w, l_scaled, l_in,
+    r_blk, r_gate, r_next, r_small, r_part, l_grad, l_w, l_down, l_in,
 ):
     sections, owners, experts, cap, chunks = sizes
     group = owners // experts
@@ -57,8 +57,9 @@
         return pltpu.make_async_copy(
             w_hbm.at[:, pl.ds(pl.multiple_of(c * width, width), width)], wv.at[c], l_w.at[c])
 
-    def scaled_store(c):
-        return pltpu.make_async_copy(scaledv.at[c], scaled_hbm.at[c], l_scaled.at[c])
+    def down_store(c):
+        return pltpu.make_async_copy(
+            downv.at[c], down_hbm.at[:, pl.ds(pl.multiple_of(c * width, width), width)], l_down.at[c])
 
     def send(src, dst, s_sem, r_sem, device):
         return pltpu.make_async_remote_copy(
@@ -266,7 +267,7 @@
                 gcol[i * cap:(i + 1) * cap, :] = jnp.broadcast_to(
                     column(grecv[i, 0:1, 0:cap]), (cap, gcol.shape[1]))
             loads[4].wait()
-            held_t_ref[...] = held_ref[...].astype(F32).T.astype(BF16)
+            held_t[...] = held_ref[...].astype(F32).T.astype(BF16)
             proj[...] = jnp.zeros_like(proj)
 
         @pl.when(c3 >= 0)
@@ -276,14 +277,16 @@
             w_load(c3).wait()
             proj[...] += lax.dot_general(buf[c3], wv[c3], (((1,), (1,)), ((), ())),
                                          preferred_element_type=F32)
-            for p in range(0, width, 128):
-                scaledv[c3, :, p:p + 128] = (gcol[...] * buf[c3, :, p:p + 128].astype(F32)).astype(BF16)
-            scaled_store(c3).start()
+            scaled = jnp.concatenate(
+                [(gcol[...] * buf[c3, :, p:p + 128].astype(F32)).astype(BF16) for p in range(0, width, 128)],
+                axis=1)
+            downv[c3] = jnp.dot(held_t[...], scaled, preferred_element_type=F32).astype(BF16)
+            down_store(c3).start()
             drain(c3)
 
             @pl.when(c3 > 0)
             def _():
-                scaled_store(c3 - 1).wait()
+                down_store(c3 - 1).wait()
 
         return carry
 
@@ -299,9 +302,12 @@
         for i in range(owners):
             part_copy(i).start()
 
-    hg_ref[...] = (gcol[:, 0:1] * proj[...]).astype(BF16)
-
-    scaled_store(chunks - 1).wait()
+    hgv[...] = (gcol[:, 0:1] * proj[...]).astype(BF16)
+
+    hg_store = pltpu.make_async_copy(hgv, hg_hbm, l_in.at[0])
+    hg_store.start()
+    down_store(chunks - 1).wait()
+    hg_store.wait()
     for r, q in gate_pairs:
         gate_copy(r, q).wait_send()
 
@@ -334,22 +340,53 @@
 
 
 def finish(
-    sections, experts, held_t_ref, hg_ref, scaled_ref, logit_ref, next_ref, router_ref,
-    down_ref, hidden_ref, passed_ref,
+    sections, experts,
+    down_in, hg_in, next_in, router_ref, logit_ref,
+    down_out, hg_out, passed_out,
+    nextv, passv, l_next, l_pass, l_down, l_hg,
 ):
-    @pl.when(pl.program_id(0) == 0)
-    def _():
-        hidden_ref[...] = hg_ref[...]
-
+    chunks, toks, width = nextv.shape
+    pieces = l_down.shape[0]
+    rows = down_in.shape[0] // pieces
+
+    def load(c):
+        return pltpu.make_async_copy(next_in.at[c], nextv.at[c], l_next.at[c])
+
+    def store(c):
+        return pltpu.make_async_copy(
+            passv.at[c], passed_out.at[:, pl.ds(pl.multiple_of(c * width, width), width)], l_pass.at[c])
+
+    def move(i):
+        part = pl.ds(pl.multiple_of(i * rows, rows), rows)
+        return pltpu.make_async_copy(down_in.at[part], down_out.at[part], l_down.at[i])
+
+    def each(count, act):
+        def body(i, carry):
+            act(i)
+            return carry
+
+        lax.fori_loop(0, count, body, 0)
+
+    each(chunks, lambda c: load(c).start())
+    each(pieces, lambda i: move(i).start())
+    hg_move = pltpu.make_async_copy(hg_in, hg_out, l_hg.at[0])
+    hg_move.start()
     last = lax.axis_index("section") == sections - 1
-    for c in range(scaled_ref.shape[0]):
-        cols = slice(c * CHUNK, (c + 1) * CHUNK)
-        down_ref[:, cols] = jnp.dot(
-            held_t_ref[...], scaled_ref[c], preferred_element_type=F32).astype(BF16)
-        total = next_ref[c].astype(F32)
+
+    def form(c):
+        load(c).wait()
+        total = nextv[c].astype(F32)
+        cols = pl.ds(pl.multiple_of(c * width, width), width)
+        routers = router_ref[:, cols].astype(F32)
         for e in range(experts):
-            total = total + logit_ref[:, e:e + 1] * router_ref[e:e + 1, cols].astype(F32)
-        passed_ref[:, cols] = jnp.where(last, 0.0, total).astype(BF16)
+            total = total + logit_ref[:, e:e + 1] * routers[e:e + 1]
+        passv[c] = jnp.where(last, 0.0, total).astype(BF16)
+        store(c).start()
+
+    each(chunks, form)
+    each(chunks, lambda c: store(c).wait())
+    each(pieces, lambda i: move(i).wait())
+    hg_move.wait()
 
 
 def shards(out_grad, router_weight, down_weight, hidden_saved, slot_token, slot_count, slot_gate):
@@ -380,7 +417,9 @@
         pltpu.VMEM((chunks, hid, CHUNK), BF16),
         pltpu.VMEM((chunks, slots, CHUNK), BF16),
         pltpu.VMEM((experts - 1, chunks, cap, CHUNK), BF16),
-        pltpu.VMEM((chunks, slots, CHUNK), BF16),
+        pltpu.VMEM((chunks, hid, CHUNK), BF16),
+        pltpu.VMEM((slots, hid), BF16),
+        pltpu.VMEM((hid, slots), BF16),
         pltpu.VMEM((slots, hid), F32),
         pltpu.VMEM((experts * cap, toks), BF16),
         pltpu.VMEM((experts, 8, 128), F32),
@@ -398,49 +437,40 @@
         dma((owners, chunks)), dma((owners,)), dma((chunks,)), dma((2,)), dma((owners,)),
         dma((chunks,)), dma((chunks,)), dma((chunks,)), dma((5,)),
     ]
-    scaled, held_t, hidden_grad, following, router_next, logit = pl.pallas_call(
+    down_grad, hidden_grad, following, router_next, logit = pl.pallas_call(
         functools.partial(exchange, (sections, owners, experts, cap, chunks)),
         out_shape=(
-            shape((chunks, slots, CHUNK), BF16),
-            shape((hid, slots), BF16),
+            shape((hid, width), BF16),
             shape((slots, hid), BF16),
             shape((chunks, toks, CHUNK), BF16),
             shape((pad_r, width), BF16),
             shape((toks, 128), F32),
         ),
         in_specs=[hbm] * 7,
-        out_specs=(anyw, vmem, vmem, anyw, anyw, vmem),
+        out_specs=(anyw, anyw, anyw, anyw, vmem),
         scratch_shapes=scratch,
         compiler_params=pltpu.CompilerParams(
             collective_id=0, has_side_effects=True, vmem_limit_bytes=64 * 2**20),
         cost_estimate=pl.CostEstimate(
-            flops=2 * slots * hid * width, bytes_accessed=2 * width * (2 * toks + hid + slots),
+            flops=4 * slots * hid * width, bytes_accessed=2 * width * (2 * toks + hid + slots),
             transcendentals=0),
     )(slot_token[0, 0], slot_count[0], slot_gate[0, 0], held, router_weight[0].T, grad, w_block)
 
-    per = 2 if chunks % 2 == 0 else 1
     down_grad, hidden, passed = pl.pallas_call(
         functools.partial(finish, sections, experts),
-        grid=(chunks // per,),
         out_shape=(shape((hid, width), BF16), shape((slots, hid), BF16), shape((toks, width), BF16)),
-        in_specs=[
-            pl.BlockSpec((hid, slots), lambda k: (0, 0)),
-            pl.BlockSpec((slots, hid), lambda k: (0, 0)),
-            pl.BlockSpec((per, slots, CHUNK), lambda k: (k, 0, 0)),
-            pl.BlockSpec((toks, 128), lambda k: (0, 0)),
-            pl.BlockSpec((per, toks, CHUNK), lambda k: (k, 0, 0)),
-            pl.BlockSpec((pad_r, per * CHUNK), lambda k: (0, k)),
+        in_specs=[anyw, anyw, anyw, vmem, vmem],
+        out_specs=(anyw, anyw, anyw),
+        scratch_shapes=[
+            pltpu.VMEM((chunks, toks, CHUNK), BF16),
+            pltpu.VMEM((chunks, toks, CHUNK), BF16),
+            dma((chunks,)), dma((chunks,)), dma((8,)), dma((1,)),
         ],
-        out_specs=(
-            pl.BlockSpec((hid, per * CHUNK), lambda k: (0, k)),
-            pl.BlockSpec((slots, hid), lambda k: (0, 0)),
-            pl.BlockSpec((toks, per * CHUNK), lambda k: (0, k)),
-        ),
         compiler_params=pltpu.CompilerParams(vmem_limit_bytes=64 * 2**20),
         cost_estimate=pl.CostEstimate(
-            flops=2 * slots * hid * width, bytes_accessed=2 * width * (2 * toks + hid + slots),
+            flops=2 * toks * experts * width, bytes_accessed=4 * width * (toks + hid),
             transcendentals=0),
-    )(held_t, hidden_grad, scaled, logit, following, router_next)
+    )(down_grad, hidden_grad, following, router_next, logit)
     return down_grad[None], hidden.reshape(hidden_saved.shape), passed[None]
 
 

time: 62.8 us -> 172 us (2.74)
  Pallas kernels: 61.9 us -> 171 us
    pallas_call x1, Pallas kernels: 8.51 us -> 118 us  [shards(): pl.pallas_call(functools.partial(finish, sections, experts), out_shape=(s...]
where the time goes in v3:
time: 172 us
  Pallas kernels  171 us (99%)
    pallas_call x1, Pallas kernels, shards(): pl.pallas_call(functools.partial(finish, sections, experts), out_shape=(s...  118 us
    pallas_call x1, Pallas kernels, shards(): pl.pallas_call(functools.partial(exchange, (sections, owners, experts, ca...  53.3 us

profile of v3, /device:TPU:1, one launch (start us, length us, event | category | flops | bytes accessed | tf_op | source)
XLA Modules:
  0.0 171.5 jit_solution(4261714861142934310)
XLA Ops:
  0.6 53.3 %shard_map.94 = (bf16[256,7168]{1,0:T(8,128)(2,1)}, bf16[256,256]{1,0:T(8,128)(2,1)}, bf16[14,128,512]{2,1,0:T(8,128)(2,1)}, bf16[16,7168]{1,0:T(8,128)(2,1)}, f32[128,128]{1,0:T(8,128)}) custom-call(s32[2,32]{1,0:T(2,128)} %bitcast.19, s32[1,2]{1,0:T(1,128)} %bitcast.21, f32[2,32]{1,0:T(2,128)} %bitcast.20, bf16[256,256]{1,0:T(8,128)(2,1)} %bitcast.16, ...), custom_call_target="tpu_custom_call" | custom-call | flops 1879048192 | bytes 11010048 | tf_op jit(solution)/shard_map/pallas_call | solution.py:440
  54.0 117.5 %shard_map.95 = (bf16[256,7168]{1,0:T(8,128)(2,1)}, bf16[256,256]{1,0:T(8,128)(2,1)}, bf16[128,7168]{1,0:T(8,128)(2,1)}) custom-call(bf16[256,7168]{1,0:T(8,128)(2,1)} %get-tuple-element.11.down_in, bf16[256,256]{1,0:T(8,128)(2,1)} %get-tuple-element.12.hg_in, bf16[14,128,512]{2,1,0:T(8,128)(2,1)} %get-tuple-element.13.next_in, ...), custom_call_target="tpu_custom_call" | custom-call | flops 3670016 | bytes 11010048 | tf_op jit(solution)/shard_map/pallas_call | solution.py:459

commit v4 on v3

--- a/solution.py
+++ b/solution.py
@@ -343,7 +343,7 @@
     sections, experts,
     down_in, hg_in, next_in, router_ref, logit_ref,
     down_out, hg_out, passed_out,
-    nextv, passv, l_next, l_pass, l_down, l_hg,
+    nextv, passv, downv, hgv, l_next, l_pass, l_down, l_out, l_hg,
 ):
     chunks, toks, width = nextv.shape
     pieces = l_down.shape[0]
@@ -358,7 +358,15 @@
 
     def move(i):
         part = pl.ds(pl.multiple_of(i * rows, rows), rows)
-        return pltpu.make_async_copy(down_in.at[part], down_out.at[part], l_down.at[i])
+        return pltpu.make_async_copy(down_in.at[part], downv.at[part], l_down.at[i])
+
+    def put(i):
+        part = pl.ds(pl.multiple_of(i * rows, rows), rows)
+        return pltpu.make_async_copy(downv.at[part], down_out.at[part], l_out.at[i])
+
+    def pass_on(i):
+        move(i).wait()
+        put(i).start()
 
     def each(count, act):
         def body(i, carry):
@@ -367,10 +375,12 @@
 
         lax.fori_loop(0, count, body, 0)
 
+    each(pieces, lambda i: move(i).start())
     each(chunks, lambda c: load(c).start())
-    each(pieces, lambda i: move(i).start())
-    hg_move = pltpu.make_async_copy(hg_in, hg_out, l_hg.at[0])
+    hg_move = pltpu.make_async_copy(hg_in, hgv, l_hg.at[0])
+    hg_put = pltpu.make_async_copy(hgv, hg_out, l_hg.at[1])
     hg_move.start()
+    each(pieces, pass_on)
     last = lax.axis_index("section") == sections - 1
 
     def form(c):
@@ -384,9 +394,11 @@
         store(c).start()
 
     each(chunks, form)
+    hg_move.wait()
+    hg_put.start()
     each(chunks, lambda c: store(c).wait())
-    each(pieces, lambda i: move(i).wait())
-    hg_move.wait()
+    each(pieces, lambda i: put(i).wait())
+    hg_put.wait()
 
 
 def shards(out_grad, router_weight, down_weight, hidden_saved, slot_token, slot_count, slot_gate):
@@ -464,7 +476,9 @@
         scratch_shapes=[
             pltpu.VMEM((chunks, toks, CHUNK), BF16),
             pltpu.VMEM((chunks, toks, CHUNK), BF16),
-            dma((chunks,)), dma((chunks,)), dma((8,)), dma((1,)),
+            pltpu.VMEM((hid, width), BF16),
+            pltpu.VMEM((slots, hid), BF16),
+            dma((chunks,)), dma((chunks,)), dma((8,)), dma((8,)), dma((2,)),
         ],
         compiler_params=pltpu.CompilerParams(vmem_limit_bytes=64 * 2**20),
         cost_estimate=pl.CostEstimate(

time: 172 us -> 60.4 us (0.35)
  Pallas kernels: 171 us -> 59.6 us
    pallas_call x1, Pallas kernels: 118 us -> 6.23 us  [shards(): pl.pallas_call(functools.partial(finish, sections, experts), out_shape=(s...]
where the time goes in v4:
time: 60.4 us; the launch traced here: 60.2 us
  Pallas kernels  59.6 us (99%)
  between operations  0.64 us (1%)
    pallas_call x1, Pallas kernels, shards(): pl.pallas_call(functools.partial(exchange, (sections, owners, experts, ca...  53.3 us
    pallas_call x1, Pallas kernels, shards(): pl.pallas_call(functools.partial(finish, sections, experts), out_shape=(s...  6.23 us

profile of v4, /device:TPU:1, one launch (start us, length us, event | category | flops | bytes accessed | tf_op | source)
XLA Modules:
  0.0 60.2 jit_solution(2524194714077256044)
XLA Ops:
  0.6 53.3 %shard_map.94 = (bf16[256,7168]{1,0:T(8,128)(2,1)}, bf16[256,256]{1,0:T(8,128)(2,1)}, bf16[14,128,512]{2,1,0:T(8,128)(2,1)}, bf16[16,7168]{1,0:T(8,128)(2,1)}, f32[128,128]{1,0:T(8,128)}) custom-call(s32[2,32]{1,0:T(2,128)} %bitcast.19, s32[1,2]{1,0:T(1,128)} %bitcast.21, f32[2,32]{1,0:T(2,128)} %bitcast.20, bf16[256,256]{1,0:T(8,128)(2,1)} %bitcast.16, ...), custom_call_target="tpu_custom_call" | custom-call | flops 1879048192 | bytes 11010048 | tf_op jit(solution)/shard_map/pallas_call | solution.py:452
  54.0 6.2 %shard_map.95 = (bf16[256,7168]{1,0:T(8,128)(2,1)}, bf16[256,256]{1,0:T(8,128)(2,1)}, bf16[128,7168]{1,0:T(8,128)(2,1)}) custom-call(bf16[256,7168]{1,0:T(8,128)(2,1)} %get-tuple-element.11.down_in, bf16[256,256]{1,0:T(8,128)(2,1)} %get-tuple-element.12.hg_in, bf16[14,128,512]{2,1,0:T(8,128)(2,1)} %get-tuple-element.13.next_in, ...), custom_call_target="tpu_custom_call" | custom-call | flops 3670016 | bytes 11010048 | tf_op jit(solution)/shard_map/pallas_call | solution.py:471
